TPU v7x, 512 devices: a whole 4x4x16 slice. The times are simulated.
512 devices in a mesh: zone: 32 (over z, core), line: 16 (over y, x).
Axes of the slice: x: 4, y: 4, z: 16, core: 2. Of those that a mesh axis runs over, the one named last changes fastest.
Arguments:
- flow_state: float32 [32, 5, 64, 128, 128], P('zone', None, 'line'), may hold values from -6 to 6
- derivative: float32 [2, 128, 128], replicated, may hold values from -0.5 to 0.5
- derivative_z: float32 [64, 64], replicated, may hold values from -0.75 to 0.75
- line_inverse: float32 [32, 2, 5, 128, 128], P('zone')
- line_inverse_z: float32 [32, 5, 64, 64], P('zone')
- mixers: float32 [32, 7, 5, 5], P('zone')
- zone_size: int32 [32], P('zone'), may hold values from 1 to 64, 682 in all
- receiver_line: int32 [32, 16, 128], P('zone', 'line'), may hold values from 0 to 511, as said below
- donor_group: int32 [32, 16, 128, 1], P('zone', 'line'), may hold values from 0 to 31; in each aligned block of 128 rows (0 to 127, 128 to 255, ..., all dimensions but the last counted through in order) at most 10 rows name the same one
- donor_line: int32 [32, 16, 128, 2], P('zone', 'line'), may hold values from 0 to 511
- stencil_weight: float32 [32, 16, 128], P('zone', 'line'), may hold values from 0 to 1
Outputs:
- state_update: float32 [32, 5, 64, 128, 128], P('zone', None, 'line')
Inputs may be any that keep to these rules, and one draw needn't show every extreme that they name: `receiver_line`: within one line block of one group the 128 receiver lines are distinct. `donor_group`: among the 128 slots of one line block of one group no donor group is named more than 10 times; in some line blocks some donor group is named exactly 10 times. `zone_size`: the sizes of all groups add up to 682, and the largest is 64.
All inputs are finite; a program needn't handle non-finite values.
Results may differ from a plain program's by a relative error of at most 0.0003.
Values sent between devices are 32-bit elements; how exact they have to be, the bound alone decides.
A program may use at most 64 MiB of HBM per device.

v0:
```python
import functools

import jax
import jax.numpy as jnp
from jax import lax
from jax.experimental import pallas as pl
from jax.experimental.pallas import tpu as pltpu
from jax.sharding import PartitionSpec as P

f32 = jnp.float32
bf16 = jnp.bfloat16
VARS = 5
LANES = 128
CHUNKS = ((0, 2), (2, 4), (4, 5))


def split(x):
    high = x.astype(bf16)
    return high, (x - high.astype(f32)).astype(bf16)


def dot(a, b):
    return jnp.dot(a, b, preferred_element_type=f32)


def left_rows(w):
    high, low = split(w)
    return jnp.concatenate(
        [jnp.concatenate([high, high], 1), jnp.concatenate([low, jnp.zeros_like(low)], 1)], 0
    )


def left_mul(w, x):
    high, low = split(x)
    both = dot(left_rows(w), jnp.concatenate([high, low], 0))
    half = w.shape[0]
    return both[:half] + both[half:]


def right_columns(w):
    high, low = split(w)
    return jnp.concatenate(
        [jnp.concatenate([high, low], 1), jnp.concatenate([high, jnp.zeros_like(low)], 1)], 0
    )


def right_mul(x, columns):
    high, low = split(x)
    both = dot(jnp.concatenate([high, low], 1), columns)
    half = columns.shape[1] // 2
    return both[:, :half] + both[:, half:]


def pick(rows, x):
    first, rest = split(x)
    rest = x - first.astype(f32)
    second = rest.astype(bf16)
    third = (rest - second.astype(f32)).astype(bf16)
    return (dot(rows, first) + dot(rows, second)) + dot(rows, third)


def iota(shape, axis):
    return lax.broadcasted_iota(jnp.int32, shape, axis)


def kernel(
    capacity,
    q, deriv, deriv_z, inverse, inverse_z, mix, size, receivers, donors, pairs, weights,
    out,
    req_out, req_in, q_strips, q_both, q_turned, ddx, ddy, part, part_strips, ret_out, ret_in, choose, place,
    part_turned, zed, mixed, solved, turned_back, back, step_a, step_b,
    local_sem, req_sem, q_sem, ret_send, ret_recv, part_send, part_recv, back_send, back_recv,
):
    groups, blocks = lax.axis_size("zone"), lax.axis_size("line")
    zone, line = lax.axis_index("zone"), lax.axis_index("line")
    planes, edge = q.shape[1], q.shape[2]
    rows = planes * edge
    depth = planes * blocks
    width = edge // blocks
    slots = receivers.shape[1]
    piece = planes * width
    named = groups * capacity
    padded = ret_in.shape[1]

    def over_zone(body):
        def step(s, carry):
            body(lax.rem(zone + s, groups))
            return carry

        lax.fori_loop(1, groups, step, 0)

    def over_line(body):
        def step(s, carry):
            body(lax.rem(line + s, blocks))
            return carry

        lax.fori_loop(1, blocks, step, 0)

    def strips(x):
        x = x.reshape(planes, blocks, width, LANES)
        return jnp.swapaxes(x, 0, 1).reshape(blocks, piece, LANES)

    def level(t):
        return pl.ds(pl.multiple_of(t * piece, piece), piece)

    others = pl.ds(0, (blocks - 1) * piece)

    def wait_for(ref, sem):
        pltpu.make_async_copy(ref, ref, sem).wait()

    barrier = pltpu.get_barrier_semaphore()
    over_zone(lambda g: pl.semaphore_signal(barrier, inc=1, device_id={"zone": g}))
    over_line(lambda t: pl.semaphore_signal(barrier, inc=1, device_id={"line": t}))

    diagonal = iota((slots, slots), 0) == iota((slots, slots), 1)

    def column(row):
        return jnp.sum(jnp.where(diagonal, row, 0.0), axis=1, keepdims=True)

    donor_row = donors[...].astype(f32)
    donor = column(donor_row)
    same_before = (donor == donor_row) & (iota((slots, slots), 1) < iota((slots, slots), 0))
    position = jnp.sum(jnp.where(same_before, 1.0, 0.0), axis=1, keepdims=True)
    lane = iota((slots, LANES), 1).astype(f32)
    line_pair = pairs[...].astype(f32)
    told = (
        jnp.where(lane == position, column(line_pair[0:1]), 0.0)
        + jnp.where(lane == position + capacity, column(line_pair[1:2]), 0.0)
        + jnp.where(lane == position + 2 * capacity, column(weights[...]), 0.0)
    )
    asks = jnp.where(iota((groups, slots), 0).astype(f32) == donor_row, 1.0, 0.0).astype(bf16)
    req_out[...] = pick(asks, told).reshape(groups, 1, LANES)

    pl.semaphore_wait(barrier, groups + blocks - 2)

    def send_request(g):
        pltpu.make_async_remote_copy(
            src_ref=req_out.at[g], dst_ref=req_in.at[zone],
            send_sem=req_sem.at[0], recv_sem=req_sem.at[1], device_id={"zone": g},
        ).start()

    over_zone(send_request)
    own_request = pltpu.make_async_copy(req_out.at[zone], req_in.at[zone], local_sem.at[0])
    own_request.start()

    def cut_state(v, carry):
        q_strips[v] = strips(q[v])
        return carry

    lax.fori_loop(0, VARS, cut_state, 0)

    def send_state(t):
        pltpu.make_async_remote_copy(
            src_ref=q_strips.at[:, t], dst_ref=q_turned.at[:, level(line)],
            send_sem=q_sem.at[0], recv_sem=q_sem.at[1], device_id={"line": t},
        ).start()

    over_line(send_state)
    own_state = pltpu.make_async_copy(
        q_strips.at[:, line], q_turned.at[:, level(line)], local_sem.at[1]
    )
    own_state.start()

    def part_state(v, carry):
        high, low = split(q[v].reshape(rows, LANES))
        q_both[v] = jnp.concatenate([high, low], 1)
        return carry

    lax.fori_loop(0, VARS, part_state, 0)

    own_request.wait()
    wait_for(req_in.at[pl.ds(0, groups - 1)], req_sem.at[1])
    slot = iota((named, groups), 0)
    low_end = iota((named, groups), 1) * capacity
    spread = jnp.where((slot >= low_end) & (slot < low_end + capacity), 1.0, 0.0).astype(bf16)
    asked = pick(spread, req_in[...].reshape(groups, LANES))
    slot = iota((named, LANES), 0)
    turn = slot - capacity * ((slot * (65536 // capacity + 1)) >> 16)
    lane = iota((named, LANES), 1)

    def field(n):
        return jnp.sum(jnp.where(lane == turn + n * capacity, asked, 0.0), axis=1, keepdims=True)

    first_line, second_line, share = field(0), field(1), field(2)
    cell_line = iota((named, rows), 1).astype(f32)
    high, low = split(
        jnp.where(cell_line == first_line, share, 0.0)
        + jnp.where(cell_line == second_line, 1.0 - share, 0.0)
    )
    choose[0:named] = high
    choose[named:] = low

    def interpolate(v, carry):
        both = dot(choose[...], q_both[v])
        value = (both[:named, :LANES] + both[:named, LANES:]) + both[named:, :LANES]
        ret_out[v] = value.reshape(named, 1, LANES)
        return carry

    own_lines = []
    for c, (start, stop) in enumerate(CHUNKS):
        lax.fori_loop(start, stop, interpolate, 0)

        def send_lines(g):
            pltpu.make_async_remote_copy(
                src_ref=ret_out.at[start:stop, pl.ds(g * capacity, capacity)],
                dst_ref=ret_in.at[start:stop, pl.ds(zone * capacity, capacity)],
                send_sem=ret_send.at[c], recv_sem=ret_recv.at[c], device_id={"zone": g},
            ).start()

        over_zone(send_lines)
        mine = pl.ds(zone * capacity, capacity)
        copy = pltpu.make_async_copy(
            ret_out.at[start:stop, mine], ret_in.at[start:stop, mine], local_sem.at[2 + c]
        )
        copy.start()
        own_lines.append(copy)

    first_columns = right_columns(deriv[0].T)
    second_rows = left_rows(deriv[1])

    def derive(v, carry):
        both = dot(q_both[v], first_columns)
        ddx[v] = both[:, :LANES] + both[:, LANES:]
        state = q_both[v]
        stacked = jnp.concatenate(
            [
                jnp.concatenate([state[k * edge:(k + 1) * edge, n:n + LANES] for k in range(planes)], 1)
                for n in (0, LANES)
            ],
            0,
        )
        both = dot(second_rows, stacked)
        both = both[:edge] + both[edge:]
        for k in range(planes):
            ddy[v, k * edge:(k + 1) * edge] = both[:, k * LANES:(k + 1) * LANES]
        return carry

    lax.fori_loop(0, VARS, derive, 0)
    tile = min(32, edge)

    def residual(n, carry):
        at = pl.ds(pl.multiple_of(n * tile, tile), tile)
        plane = n // (edge // tile)
        active = line * planes + plane < size[0]
        x = [ddx[v, at] for v in range(VARS)]
        y = [ddy[v, at] for v in range(VARS)]
        for a in range(VARS):
            total = mix[0, a, 0] * x[0] + mix[1, a, 0] * y[0]
            for v in range(1, VARS):
                total += mix[0, a, v] * x[v] + mix[1, a, v] * y[v]
            part[a, at] = jnp.where(active, -total, 0.0)
        return carry

    lax.fori_loop(0, rows // tile, residual, 0)

    slot_of = donor * capacity + position
    here = jnp.sum(
        jnp.where(
            iota((slots, padded), 1).astype(f32) == slot_of,
            column(receivers[...].astype(f32)) + 1.0,
            0.0,
        ),
        axis=0,
        keepdims=True,
    ) - 1.0
    place[...] = jnp.where(iota((rows, padded), 0).astype(f32) == here, 1.0, 0.0).astype(bf16)
    is_receiver = jnp.sum(
        jnp.where(iota((rows, slots), 0) == receivers[...], 1.0, 0.0), axis=1, keepdims=True
    )
    if padded > named:
        ret_in[:, named:] = jnp.zeros((VARS, padded - named, 1, LANES), f32)

    own_state.wait()
    wait_for(q_turned.at[:, others], q_sem.at[1])

    def whole_lines(ref, v):
        return jnp.concatenate(
            [ref[v, pl.ds(j, depth, stride=width), :] for j in range(width)], 1
        )

    def derive_z(v, carry):
        zed[v] = left_mul(deriv_z[...], whole_lines(q_turned, v))
        return carry

    lax.fori_loop(0, VARS, derive_z, 0)
    active_all = iota((depth, LANES), 0) < size[0]

    def residual_z(j, carry):
        at = pl.ds(pl.multiple_of(j * LANES, LANES), LANES)
        z = [zed[v, :, at] for v in range(VARS)]
        for a in range(VARS):
            total = mix[2, a, 0] * z[0]
            for v in range(1, VARS):
                total += mix[2, a, v] * z[v]
            mixed[a, :, at] = jnp.where(active_all, -total, 0.0)
        return carry

    lax.fori_loop(0, width, residual_z, 0)

    def add_source(v, carry):
        high, low = split(ret_in[v].reshape(padded, LANES))
        both = dot(place[...], jnp.concatenate([high, low], 1))
        own = is_receiver * q[v].reshape(rows, LANES)
        part_strips[v] = strips(part[v] + (both[:, :LANES] + both[:, LANES:] - own))

        def send_part(t):
            pltpu.make_async_remote_copy(
                src_ref=part_strips.at[v, t],
                dst_ref=part_turned.at[v, level(line)],
                send_sem=part_send.at[v], recv_sem=part_recv.at[v], device_id={"line": t},
            ).start()

        over_line(send_part)
        part_turned[v, level(line)] = part_strips[v, line]
        return carry

    for c, (start, stop) in enumerate(CHUNKS):
        own_lines[c].wait()
        wait_for(ret_in.at[start:stop, pl.ds(0, named - capacity)], ret_recv.at[c])
        lax.fori_loop(start, stop, add_source, 0)

    for v in range(VARS):
        wait_for(part_turned.at[v, others], part_recv.at[v])

    def to_first(j, carry):
        at = pl.ds(pl.multiple_of(j * LANES, LANES), LANES)
        r = [part_turned[v, pl.ds(j, depth, stride=width), :] + mixed[v, :, at] for v in range(VARS)]
        for a in range(VARS):
            total = mix[3, a, 0] * r[0]
            for v in range(1, VARS):
                total += mix[3, a, v] * r[v]
            zed[a, :, at] = total
        return carry

    lax.fori_loop(0, width, to_first, 0)

    def solve_z(v, carry):
        solved[v] = left_mul(inverse_z[v], zed[v])
        return carry

    lax.fori_loop(0, VARS, solve_z, 0)

    def send_back(a, carry):
        for j in range(width):
            at = slice(j * LANES, (j + 1) * LANES)
            total = mix[4, a, 0] * solved[0, :, at]
            for v in range(1, VARS):
                total += mix[4, a, v] * solved[v, :, at]
            turned_back[a, pl.ds(j, depth, stride=width), :] = total

        def send(t):
            pltpu.make_async_remote_copy(
                src_ref=turned_back.at[a, level(t)],
                dst_ref=back.at[a, line],
                send_sem=back_send.at[a], recv_sem=back_recv.at[a], device_id={"line": t},
            ).start()

        over_line(send)
        back[a, line] = turned_back[a, level(line)]
        return carry

    lax.fori_loop(0, VARS, send_back, 0)

    def plane_of(v, k):
        return back[v, :, k * width:(k + 1) * width, :].reshape(edge, LANES)

    def solve_y(v, carry):
        wait_for(turned_back.at[v, others], back_recv.at[v])
        both = left_mul(inverse[1, v], jnp.concatenate([plane_of(v, k) for k in range(planes)], 1))
        for k in range(planes):
            step_a[v, k * edge:(k + 1) * edge] = both[:, k * LANES:(k + 1) * LANES]
        return carry

    lax.fori_loop(0, VARS, solve_y, 0)

    def mix_over(m, source, store):
        def body(n, carry):
            at = pl.ds(pl.multiple_of(n * tile, tile), tile)
            x = [source[v, at] for v in range(VARS)]
            for a in range(VARS):
                total = mix[m, a, 0] * x[0]
                for v in range(1, VARS):
                    total += mix[m, a, v] * x[v]
                store(a, n, at, total)
            return carry

        lax.fori_loop(0, rows // tile, body, 0)

    def keep(a, n, at, total):
        step_b[a, at] = total

    def give(a, n, at, total):
        inside = lax.rem(n, edge // tile) * tile
        out[a, n // (edge // tile), pl.ds(pl.multiple_of(inside, tile), tile)] = total

    mix_over(5, step_a, keep)

    def solve_x(v, carry):
        step_a[v] = right_mul(step_b[v], right_columns(inverse[0, v].T))
        return carry

    lax.fori_loop(0, VARS, solve_x, 0)
    mix_over(6, step_a, give)

    wait_for(req_in.at[pl.ds(0, groups - 1)], req_sem.at[0])
    wait_for(q_turned.at[:, others], q_sem.at[0])
    for c, (start, stop) in enumerate(CHUNKS):
        wait_for(ret_out.at[start:stop, pl.ds(0, named - capacity)], ret_send.at[c])
    for v in range(VARS):
        wait_for(part_turned.at[v, others], part_send.at[v])
        wait_for(turned_back.at[v, others], back_send.at[v])


def local(
    flow_state, derivative, derivative_z, line_inverse, line_inverse_z, mixers, zone_size,
    receiver_line, donor_group, donor_line, stencil_weight,
):
    groups, blocks = lax.axis_size("zone"), lax.axis_size("line")
    planes, edge = flow_state.shape[2], flow_state.shape[3]
    slots = receiver_line.shape[2]
    capacity = max(2, 5 * slots // (2 * groups))
    rows, depth, width = planes * edge, planes * blocks, edge // blocks
    named = groups * capacity
    padded = -(-named // LANES) * LANES
    dma = pltpu.SemaphoreType.DMA
    vmem = pl.BlockSpec(memory_space=pltpu.VMEM)
    smem = pl.BlockSpec(memory_space=pltpu.SMEM)
    result = pl.pallas_call(
        functools.partial(kernel, capacity),
        out_shape=jax.ShapeDtypeStruct((VARS, planes, edge, LANES), f32),
        in_specs=[vmem] * 5 + [smem] * 2 + [vmem] * 4,
        out_specs=vmem,
        scratch_shapes=[
            pltpu.VMEM((groups, 1, LANES), f32),
            pltpu.VMEM((groups, 1, LANES), f32),
            pltpu.VMEM((VARS, blocks, planes * width, LANES), f32),
            pltpu.VMEM((VARS, rows, 2 * LANES), bf16),
            pltpu.VMEM((VARS, depth * width, LANES), f32),
            pltpu.VMEM((VARS, rows, LANES), f32),
            pltpu.VMEM((VARS, rows, LANES), f32),
            pltpu.VMEM((VARS, rows, LANES), f32),
            pltpu.VMEM((VARS, blocks, planes * width, LANES), f32),
            pltpu.VMEM((VARS, named, 1, LANES), f32),
            pltpu.VMEM((VARS, padded, 1, LANES), f32),
            pltpu.VMEM((2 * named, rows), bf16),
            pltpu.VMEM((rows, padded), bf16),
            pltpu.VMEM((VARS, depth * width, LANES), f32),
            pltpu.VMEM((VARS, depth, width * LANES), f32),
            pltpu.VMEM((VARS, depth, width * LANES), f32),
            pltpu.VMEM((VARS, depth, width * LANES), f32),
            pltpu.VMEM((VARS, depth * width, LANES), f32),
            pltpu.VMEM((VARS, blocks, planes * width, LANES), f32),
            pltpu.VMEM((VARS, rows, LANES), f32),
            pltpu.VMEM((VARS, rows, LANES), f32),
            dma((2 + len(CHUNKS),)),
            dma((2,)),
            dma((2,)),
            dma((len(CHUNKS),)),
            dma((len(CHUNKS),)),
            dma((VARS,)),
            dma((VARS,)),
            dma((VARS,)),
            dma((VARS,)),
        ],
        compiler_params=pltpu.CompilerParams(
            collective_id=0, has_side_effects=True, vmem_limit_bytes=48 * 2**20
        ),
    )(
        flow_state[0], derivative, derivative_z, line_inverse[0], line_inverse_z[0], mixers[0],
        zone_size, receiver_line[0], donor_group[0, :, :, 0], donor_line[0, 0].T,
        stencil_weight[0],
    )
    return result[None]


def solution(mesh):
    placed = (
        P("zone", None, "line", None, None),
        P(),
        P(),
        P("zone", None, None, None, None),
        P("zone", None, None, None),
        P("zone", None, None, None),
        P("zone"),
        P("zone", "line", None),
        P("zone", "line", None, None),
        P("zone", "line", None, None),
        P("zone", "line", None),
    )
    return jax.shard_map(
        local,
        mesh=mesh,
        in_specs=placed,
        out_specs=P("zone", None, "line", None, None),
        check_vma=False,
    )
```

profile of v0, /device:TPU:1, one launch (start us, length us, event | category | flops | bytes accessed | tf_op | source)
XLA Modules:
  0.0 106.5 jit_solution(10704670919917111794)
XLA Ops:
  0.7 0.8 copy.12
  1.5 0.0 copy-start
  1.5 1.3 %copy-done = f32[1,5,4,128,128]{4,3,2,1,0:T(8,128)S(1)} copy-done((f32[1,5,4,128,128]{4,3,2,1,0:T(8,128)S(1)}, f32[1,5,4,128,128]{4,3,2,1,0:T(8,128)}, u32[]{:S(2)}) %copy-start) | copy-done | bytes 1310744
  2.8 0.0 copy-start.1
  2.8 1.1 %copy-done.1 = f32[1,2,5,128,128]{4,3,2,1,0:T(8,128)S(1)} copy-done((f32[1,2,5,128,128]{4,3,2,1,0:T(8,128)S(1)}, f32[1,2,5,128,128]{4,3,2,1,0:T(8,128)}, u32[]{:S(2)}) %copy-start.1) | copy-done | bytes 655384
  3.9 0.0 copy-start.2
  3.9 0.9 copy-done.2
  4.8 0.0 copy-start.3
  4.8 0.9 copy-done.3
  5.7 0.0 copy-start.4
  5.7 0.8 copy-done.4
  6.5 0.0 copy-start.5
  6.5 0.7 copy-done.5
  7.2 0.0 copy-start.6
  7.2 0.7 copy-done.6
  7.8 0.0 copy-start.7
  7.8 0.7 copy-done.7
  8.5 0.0 copy-start.8
  8.5 0.7 copy-done.8
  9.1 96.3 %shard_map.109 = f32[5,4,128,128]{3,2,1,0:T(8,128)S(1)} custom-call(f32[5,4,128,128]{3,2,1,0:T(8,128)S(1)} %bitcast.12, f32[2,128,128]{2,1,0:T(8,128)S(1)} %copy-done.3, f32[64,64]{1,0:T(8,128)S(1)} %copy-done.4, f32[2,5,128,128]{3,2,1,0:T(8,128)S(1)} %bitcast.13, f32[5,64,64]{2,1,0:T(8,128)S(1)} %bitcast.14, f32[7,5,5]{2,1,0:T(8,128)S(1)} %bitcast.15, ...), custom_call_target="tpu_custom_call" | custom-call | tf_op jit(solution)/shard_map/pallas_call | solution.py:428
  105.5 1.1 copy.15
Async XLA Ops:
  1.5 1.3 %copy-start = (f32[1,5,4,128,128]{4,3,2,1,0:T(8,128)S(1)}, f32[1,5,4,128,128]{4,3,2,1,0:T(8,128)}, u32[]{:S(2)}) copy-start(f32[1,5,4,128,128]{4,3,2,1,0:T(8,128)} %param.11) | copy-start | bytes 3932164
  2.8 1.1 %copy-start.1 = (f32[1,2,5,128,128]{4,3,2,1,0:T(8,128)S(1)}, f32[1,2,5,128,128]{4,3,2,1,0:T(8,128)}, u32[]{:S(2)}) copy-start(f32[1,2,5,128,128]{4,3,2,1,0:T(8,128)} %param.14) | copy-start | bytes 1966084
  3.9 0.9 copy-start.2
  4.8 0.9 copy-start.3
  5.7 0.8 copy-start.4
  6.5 0.7 copy-start.5
  7.2 0.7 copy-start.6
  7.8 0.7 copy-start.7
  8.5 0.7 copy-start.8
where the time goes:
time: 107 us
  Pallas kernels  96.3 us (90%)
  local copies, waits for them, and re-layouts  9.52 us (9%)
    pallas_call x1, Pallas kernels, local(): pl.pallas_call(functools.partial(kernel, capacity), out_shape=jax.ShapeDt...  96.3 us
    unnamed x20, local copies, waits for them, and re-layouts  9.52 us

commit v1 on v0

v1 whole, which is shorter than its diff:
```python
import functools

import jax
import jax.numpy as jnp
from jax import lax
from jax.experimental import pallas as pl
from jax.experimental.pallas import tpu as pltpu
from jax.sharding import PartitionSpec as P

f32 = jnp.float32
bf16 = jnp.bfloat16
VARS = 5
LANES = 128


def split(x):
    high = x.astype(bf16)
    return high, (x - high.astype(f32)).astype(bf16)


def dot(a, b):
    return jnp.dot(a, b, preferred_element_type=f32)


def left_rows(w):
    high, low = split(w)
    return jnp.concatenate(
        [jnp.concatenate([high, high], 1), jnp.concatenate([low, jnp.zeros_like(low)], 1)], 0
    )


def left_mul(w, x):
    high, low = split(x)
    both = dot(left_rows(w), jnp.concatenate([high, low], 0))
    half = w.shape[0]
    return both[:half] + both[half:]


def right_columns(w):
    high, low = split(w)
    return jnp.concatenate(
        [jnp.concatenate([high, low], 1), jnp.concatenate([high, jnp.zeros_like(low)], 1)], 0
    )


def right_mul(x, columns):
    high, low = split(x)
    both = dot(jnp.concatenate([high, low], 1), columns)
    half = columns.shape[1] // 2
    return both[:, :half] + both[:, half:]


def pick(rows, x):
    first, rest = split(x)
    rest = x - first.astype(f32)
    second = rest.astype(bf16)
    third = (rest - second.astype(f32)).astype(bf16)
    return (dot(rows, first) + dot(rows, second)) + dot(rows, third)


def iota(shape, axis):
    return lax.broadcasted_iota(jnp.int32, shape, axis)


def kernel(
    capacity,
    q_hbm, deriv_hbm, deriv_z_hbm, inverse_hbm, inverse_z_hbm, mixers, size,
    receivers_hbm, donors_hbm, pairs_hbm, weights_hbm,
    out,
    q, deriv, deriv_z, inverse, inverse_z, receivers, donors, pairs, weights,
    req_out, req_in, q_strips, q_both, q_turned, ddx, ddy, part, part_strips, is_receiver,
    lines, ret_out, ret_in, choose, place,
    part_turned, zed, mixed, turned_back, back, step_a, step_b,
    load_sem, local_sem, req_sem, q_sem,
    ret_send, ret_recv, part_send, part_recv, back_send, back_recv,
):
    groups, blocks = lax.axis_size("zone"), lax.axis_size("line")
    zone, line = lax.axis_index("zone"), lax.axis_index("line")

    def mix(m, a, v):
        return mixers[a * VARS + v, 0, m]

    moves = [
        pltpu.make_async_copy(source, target, load_sem.at[n])
        for n, (source, target) in enumerate((
            (donors_hbm, donors), (pairs_hbm, pairs), (weights_hbm, weights), (q_hbm, q),
            (receivers_hbm, receivers), (deriv_hbm, deriv), (deriv_z_hbm, deriv_z),
            (inverse_z_hbm, inverse_z), (inverse_hbm, inverse),
        ))
    ]
    for move in moves:
        move.start()
    planes, edge = q.shape[1], q.shape[2]
    rows = planes * edge
    depth = planes * blocks
    width = edge // blocks
    slots = receivers.shape[1]
    piece = planes * width
    named = groups * capacity
    padded = ret_in.shape[1]

    def over_zone(body):
        def step(s, carry):
            body(lax.rem(zone + s, groups))
            return carry

        lax.fori_loop(1, groups, step, 0)

    def over_line(body):
        def step(s, carry):
            body(lax.rem(line + s, blocks))
            return carry

        lax.fori_loop(1, blocks, step, 0)

    def strips(x):
        x = x.reshape(planes, blocks, width, LANES)
        return jnp.swapaxes(x, 0, 1).reshape(blocks, piece, LANES)

    def level(t):
        return pl.ds(pl.multiple_of(t * piece, piece), piece)

    others = pl.ds(0, (blocks - 1) * piece)

    def wait_for(ref, sem):
        pltpu.make_async_copy(ref, ref, sem).wait()

    barrier = pltpu.get_barrier_semaphore()
    over_zone(lambda g: pl.semaphore_signal(barrier, inc=1, device_id={"zone": g}))
    over_line(lambda t: pl.semaphore_signal(barrier, inc=1, device_id={"line": t}))

    diagonal = iota((slots, slots), 0) == iota((slots, slots), 1)

    def column(row):
        return jnp.sum(jnp.where(diagonal, row, 0.0), axis=1, keepdims=True)

    for move in moves[:3]:
        move.wait()
    donor_row = donors[...].astype(f32)
    donor = column(donor_row)
    same_before = (donor == donor_row) & (iota((slots, slots), 1) < iota((slots, slots), 0))
    position = jnp.sum(jnp.where(same_before, 1.0, 0.0), axis=1, keepdims=True)
    lane = iota((slots, LANES), 1).astype(f32)
    line_pair = pairs[...].astype(f32)
    told = (
        jnp.where(lane == position, column(line_pair[0:1]), 0.0)
        + jnp.where(lane == position + capacity, column(line_pair[1:2]), 0.0)
        + jnp.where(lane == position + 2 * capacity, column(weights[...]), 0.0)
    )
    asks = jnp.where(iota((groups, slots), 0).astype(f32) == donor_row, 1.0, 0.0).astype(bf16)
    own_mixer = jnp.zeros((1, LANES), f32)
    for n in range(VARS * VARS):
        at = iota((1, LANES), 1) == 3 * capacity + n
        own_mixer = jnp.where(at, mixers[n, 0, 3], own_mixer)
    req_out[...] = (pick(asks, told) + own_mixer).reshape(groups, 1, LANES)
    moves[3].wait()

    def cut_state(v, carry):
        q_strips[v] = strips(q[v])
        return carry

    lax.fori_loop(0, VARS, cut_state, 0)

    pl.semaphore_wait(barrier, groups + blocks - 2)

    def send_request(g):
        pltpu.make_async_remote_copy(
            src_ref=req_out.at[g], dst_ref=req_in.at[zone],
            send_sem=req_sem.at[0], recv_sem=req_sem.at[1], device_id={"zone": g},
        ).start()

    over_zone(send_request)
    own_request = pltpu.make_async_copy(req_out.at[zone], req_in.at[zone], local_sem.at[0])
    own_request.start()

    def send_state(t):
        pltpu.make_async_remote_copy(
            src_ref=q_strips.at[:, t], dst_ref=q_turned.at[:, level(line)],
            send_sem=q_sem.at[0], recv_sem=q_sem.at[1], device_id={"line": t},
        ).start()

    over_line(send_state)
    own_state = pltpu.make_async_copy(
        q_strips.at[:, line], q_turned.at[:, level(line)], local_sem.at[1]
    )
    own_state.start()

    def part_state(v, carry):
        high, low = split(q[v].reshape(rows, LANES))
        q_both[v] = jnp.concatenate([high, low], 1)
        return carry

    lax.fori_loop(0, VARS, part_state, 0)

    own_request.wait()
    wait_for(req_in.at[pl.ds(0, groups - 1)], req_sem.at[1])
    asked = req_in[...].reshape(groups, LANES)
    cell_line = iota((groups, rows), 1).astype(f32)
    for n in range(capacity):
        share = asked[:, 2 * capacity + n:2 * capacity + n + 1]
        high, low = split(
            jnp.where(cell_line == asked[:, n:n + 1], share, 0.0)
            + jnp.where(cell_line == asked[:, capacity + n:capacity + n + 1], 1.0 - share, 0.0)
        )
        choose[n * groups:(n + 1) * groups] = high
        choose[named + n * groups:named + (n + 1) * groups] = low

    def interpolate(v, carry):
        both = dot(choose[...], q_both[v])
        lines[v] = (both[:named, :LANES] + both[:named, LANES:]) + both[named:, :LANES]
        return carry

    lax.fori_loop(0, VARS, interpolate, 0)

    def returned(g):
        return pl.ds(g * capacity, capacity)

    other_lines = pl.ds(0, named - capacity)
    own_lines = []
    for a in range(VARS):
        first = 3 * capacity + a * VARS
        scale = [
            jnp.broadcast_to(asked[:, first + v:first + v + 1], (groups, LANES)) for v in range(VARS)
        ]
        for n in range(capacity):
            at = slice(n * groups, (n + 1) * groups)
            total = scale[0] * lines[0, at]
            for v in range(1, VARS):
                total += scale[v] * lines[v, at]
            ret_out[a, :, n] = total.reshape(groups, 1, LANES)

        def send_lines(g):
            pltpu.make_async_remote_copy(
                src_ref=ret_out.at[a, g], dst_ref=ret_in.at[a, returned(zone)],
                send_sem=ret_send.at[a], recv_sem=ret_recv.at[a], device_id={"zone": g},
            ).start()

        over_zone(send_lines)
        copy = pltpu.make_async_copy(
            ret_out.at[a, zone], ret_in.at[a, returned(zone)], local_sem.at[2 + a]
        )
        copy.start()
        own_lines.append(copy)

    moves[4].wait()
    slot_of = donor * capacity + position
    here = jnp.sum(
        jnp.where(
            iota((slots, padded), 1).astype(f32) == slot_of,
            column(receivers[...].astype(f32)) + 1.0,
            0.0,
        ),
        axis=0,
        keepdims=True,
    ) - 1.0
    place[...] = jnp.where(iota((rows, padded), 0).astype(f32) == here, 1.0, 0.0).astype(bf16)
    is_receiver[...] = jnp.broadcast_to(
        jnp.sum(
            jnp.where(iota((rows, slots), 0) == receivers[...], 1.0, 0.0), axis=1, keepdims=True
        ),
        (rows, LANES),
    )
    if padded > named:
        ret_in[:, named:] = jnp.zeros((VARS, padded - named, 1, LANES), f32)

    moves[5].wait()
    first_columns = right_columns(deriv[0].T)
    second_rows = left_rows(deriv[1])

    def derive(v, carry):
        both = dot(q_both[v], first_columns)
        ddx[v] = both[:, :LANES] + both[:, LANES:]
        state = q_both[v]
        stacked = jnp.concatenate(
            [
                jnp.concatenate([state[k * edge:(k + 1) * edge, n:n + LANES] for k in range(planes)], 1)
                for n in (0, LANES)
            ],
            0,
        )
        both = dot(second_rows, stacked)
        both = both[:edge] + both[edge:]
        for k in range(planes):
            ddy[v, k * edge:(k + 1) * edge] = both[:, k * LANES:(k + 1) * LANES]
        return carry

    lax.fori_loop(0, VARS, derive, 0)
    tile = min(32, edge)

    def mix_of(m, a, x):
        total = mix(m, a, 0) * x[0]
        for v in range(1, VARS):
            total += mix(m, a, v) * x[v]
        return total

    def residual(n, carry):
        at = pl.ds(pl.multiple_of(n * tile, tile), tile)
        plane = n // (edge // tile)
        inside = pl.ds(pl.multiple_of(lax.rem(n, edge // tile) * tile, tile), tile)
        active = line * planes + plane < size[0]
        x = [ddx[v, at] for v in range(VARS)]
        y = [ddy[v, at] for v in range(VARS)]
        taken = is_receiver[at]
        r = [
            jnp.where(active, -(mix_of(0, a, x) + mix_of(1, a, y)), 0.0) - taken * q[a, plane, inside]
            for a in range(VARS)
        ]
        for a in range(VARS):
            part[a, at] = mix_of(3, a, r)
        return carry

    lax.fori_loop(0, rows // tile, residual, 0)

    moves[6].wait()
    own_state.wait()
    wait_for(q_turned.at[:, others], q_sem.at[1])

    def whole_lines(ref, v):
        return jnp.concatenate(
            [ref[v, pl.ds(j, depth, stride=width), :] for j in range(width)], 1
        )

    def derive_z(v, carry):
        zed[v] = left_mul(deriv_z[...], whole_lines(q_turned, v))
        return carry

    lax.fori_loop(0, VARS, derive_z, 0)
    levels = min(32, depth)

    def residual_z(n, carry):
        deep = lax.rem(n, depth // levels) * levels
        down = pl.ds(pl.multiple_of(deep, levels), levels)
        at = pl.ds(pl.multiple_of(n // (depth // levels) * LANES, LANES), LANES)
        active = iota((levels, LANES), 0) + deep < size[0]
        z = [zed[v, down, at] for v in range(VARS)]
        r = [jnp.where(active, -mix_of(2, a, z), 0.0) for a in range(VARS)]
        for a in range(VARS):
            mixed[a, down, at] = mix_of(3, a, r)
        return carry

    lax.fori_loop(0, width * (depth // levels), residual_z, 0)
    moves[7].wait()

    def add_source(a):
        wait_for(ret_in.at[a, other_lines], ret_recv.at[a])
        high, low = split(ret_in[a].reshape(padded, LANES))
        both = dot(place[...], jnp.concatenate([high, low], 1))
        part_strips[a] = strips(part[a] + (both[:, :LANES] + both[:, LANES:]))

        def send_part(t):
            pltpu.make_async_remote_copy(
                src_ref=part_strips.at[a, t], dst_ref=part_turned.at[a, level(line)],
                send_sem=part_send.at[a], recv_sem=part_recv.at[a], device_id={"line": t},
            ).start()

        over_line(send_part)
        part_turned[a, level(line)] = part_strips[a, line]

    def solve_z(a):
        wait_for(part_turned.at[a, others], part_recv.at[a])
        solved = left_mul(inverse_z[a], whole_lines(part_turned, a) + mixed[a])
        for j in range(width):
            turned_back[a, pl.ds(j, depth, stride=width), :] = solved[:, j * LANES:(j + 1) * LANES]

        def send_back(t):
            pltpu.make_async_remote_copy(
                src_ref=turned_back.at[a, level(t)], dst_ref=back.at[a, line],
                send_sem=back_send.at[a], recv_sem=back_recv.at[a], device_id={"line": t},
            ).start()

        over_line(send_back)
        back[a, line] = turned_back[a, level(line)]

    for copy in own_lines:
        copy.wait()
    add_source(0)

    def source_and_solve(a, carry):
        add_source(a)
        solve_z(a - 1)
        return carry

    lax.fori_loop(1, VARS, source_and_solve, 0)
    solve_z(VARS - 1)

    moves[8].wait()
    for a in range(VARS - 1):
        wait_for(turned_back.at[a, others], back_recv.at[a])
    last = VARS - 1
    strip_tile = min(4, blocks)

    def all_but_last(n, carry):
        at = pl.ds(n * strip_tile, strip_tile)
        x = [back[a, at] for a in range(last)]
        for v in range(VARS):
            total = mix(4, v, 0) * x[0]
            for a in range(1, last):
                total += mix(4, v, a) * x[a]
            step_b[v, at] = total
        return carry

    lax.fori_loop(0, blocks // strip_tile, all_but_last, 0)
    wait_for(turned_back.at[last, others], back_recv.at[last])

    def solve_y(v, carry):
        x = step_b[v] + mixers[v * VARS + last, 0, 4] * back[last]
        x = jnp.concatenate(
            [x[:, k * width:(k + 1) * width, :].reshape(edge, LANES) for k in range(planes)], 1
        )
        both = left_mul(inverse[1, v], x)
        for k in range(planes):
            step_a[v, k * edge:(k + 1) * edge] = both[:, k * LANES:(k + 1) * LANES]
        return carry

    lax.fori_loop(0, VARS, solve_y, 0)

    def mix_second(n, carry):
        at = pl.ds(pl.multiple_of(n * tile, tile), tile)
        x = [step_a[v, at] for v in range(VARS)]
        for a in range(VARS):
            ddx[a, at] = mix_of(5, a, x)
        return carry

    lax.fori_loop(0, rows // tile, mix_second, 0)

    def solve_x(v, carry):
        ddy[v] = right_mul(ddx[v], right_columns(inverse[0, v].T))
        return carry

    lax.fori_loop(0, VARS, solve_x, 0)

    def mix_last(n, carry):
        at = pl.ds(pl.multiple_of(n * tile, tile), tile)
        inside = pl.ds(pl.multiple_of(lax.rem(n, edge // tile) * tile, tile), tile)
        x = [ddy[v, at] for v in range(VARS)]
        for a in range(VARS):
            out[a, n // (edge // tile), inside] = mix_of(6, a, x)
        return carry

    lax.fori_loop(0, rows // tile, mix_last, 0)

    wait_for(req_in.at[pl.ds(0, groups - 1)], req_sem.at[0])
    wait_for(q_turned.at[:, others], q_sem.at[0])
    for a in range(VARS):
        wait_for(ret_in.at[a, other_lines], ret_send.at[a])
        wait_for(part_turned.at[a, others], part_send.at[a])
        wait_for(turned_back.at[a, others], back_send.at[a])


def local(
    flow_state, derivative, derivative_z, line_inverse, line_inverse_z, mixers, zone_size,
    receiver_line, donor_group, donor_line, stencil_weight,
):
    groups, blocks = lax.axis_size("zone"), lax.axis_size("line")
    planes, edge = flow_state.shape[2], flow_state.shape[3]
    slots = receiver_line.shape[2]
    capacity = max(2, 5 * slots // (2 * groups))
    rows, depth, width = planes * edge, planes * blocks, edge // blocks
    named = groups * capacity
    padded = -(-named // LANES) * LANES
    dma = pltpu.SemaphoreType.DMA
    vmem = pl.BlockSpec(memory_space=pltpu.VMEM)
    hbm = pl.BlockSpec(memory_space=pltpu.HBM)
    smem = pl.BlockSpec(memory_space=pltpu.SMEM)
    result = pl.pallas_call(
        functools.partial(kernel, capacity),
        out_shape=jax.ShapeDtypeStruct((VARS, planes, edge, LANES), f32),
        in_specs=[hbm] * 5 + [smem] * 2 + [hbm] * 4,
        out_specs=vmem,
        scratch_shapes=[
            pltpu.VMEM((VARS, planes, edge, LANES), f32),
            pltpu.VMEM(derivative.shape, f32),
            pltpu.VMEM(derivative_z.shape, f32),
            pltpu.VMEM(line_inverse.shape[1:], f32),
            pltpu.VMEM(line_inverse_z.shape[1:], f32),
            pltpu.VMEM((1, slots), jnp.int32),
            pltpu.VMEM((1, slots), jnp.int32),
            pltpu.VMEM((2, slots), jnp.int32),
            pltpu.VMEM((1, slots), f32),
            pltpu.VMEM((groups, 1, LANES), f32),
            pltpu.VMEM((groups, 1, LANES), f32),
            pltpu.VMEM((VARS, blocks, planes * width, LANES), f32),
            pltpu.VMEM((VARS, rows, 2 * LANES), bf16),
            pltpu.VMEM((VARS, depth * width, LANES), f32),
            pltpu.VMEM((VARS, rows, LANES), f32),
            pltpu.VMEM((VARS, rows, LANES), f32),
            pltpu.VMEM((VARS, rows, LANES), f32),
            pltpu.VMEM((VARS, blocks, planes * width, LANES), f32),
            pltpu.VMEM((rows, LANES), f32),
            pltpu.VMEM((VARS, named, LANES), f32),
            pltpu.VMEM((VARS, groups, capacity, 1, LANES), f32),
            pltpu.VMEM((VARS, padded, 1, LANES), f32),
            pltpu.VMEM((2 * named, rows), bf16),
            pltpu.VMEM((rows, padded), bf16),
            pltpu.VMEM((VARS, depth * width, LANES), f32),
            pltpu.VMEM((VARS, depth, width * LANES), f32),
            pltpu.VMEM((VARS, depth, width * LANES), f32),
            pltpu.VMEM((VARS, depth * width, LANES), f32),
            pltpu.VMEM((VARS, blocks, planes * width, LANES), f32),
            pltpu.VMEM((VARS, rows, LANES), f32),
            pltpu.VMEM((VARS, blocks, planes * width, LANES), f32),
            dma((9,)),
            dma((2 + VARS,)),
            dma((2,)),
            dma((2,)),
        ] + [dma((VARS,))] * 6,
        compiler_params=pltpu.CompilerParams(
            collective_id=0, has_side_effects=True, vmem_limit_bytes=48 * 2**20
        ),
    )(
        flow_state[0], derivative, derivative_z, line_inverse[0], line_inverse_z[0],
        jnp.transpose(mixers[0], (1, 2, 0)).reshape(VARS * VARS, 1, mixers.shape[1]),
        zone_size, receiver_line[0], donor_group[0, :, :, 0], donor_line[0, 0].T,
        stencil_weight[0],
    )
    return result[None]


def solution(mesh):
    placed = (
        P("zone", None, "line", None, None),
        P(),
        P(),
        P("zone", None, None, None, None),
        P("zone", None, None, None),
        P("zone", None, None, None),
        P("zone"),
        P("zone", "line", None),
        P("zone", "line", None, None),
        P("zone", "line", None, None),
        P("zone", "line", None),
    )
    return jax.shard_map(
        local,
        mesh=mesh,
        in_specs=placed,
        out_specs=P("zone", None, "line", None, None),
        check_vma=False,
    )
```

time: 107 us -> 98.3 us (0.919)
  Pallas kernels: 96.3 us -> 87.9 us
    pallas_call x1, Pallas kernels: 96.3 us -> 87.9 us  [local(): pl.pallas_call(functools.partial(kernel, capacity), out_shape=jax.ShapeDt...]
where the time goes in v1:
time: 98.3 us; the launch traced here: 97.9 us
  Pallas kernels  87.9 us (89%)
  local copies, waits for them, and re-layouts  9.41 us (10%)
    pallas_call x1, Pallas kernels, local(): pl.pallas_call(functools.partial(kernel, capacity), out_shape=jax.ShapeDt...  87.9 us
    unnamed x20, local copies, waits for them, and re-layouts  9.39 us

profile of v1, /device:TPU:1, one launch (start us, length us, event | category | flops | bytes accessed | tf_op | source)
XLA Modules:
  0.0 97.9 jit_solution(1369120016513515873)
XLA Ops:
  0.7 0.7 copy.18
  1.4 0.0 copy-start
  1.4 1.3 %copy-done = f32[1,5,4,128,128]{4,3,2,1,0:T(8,128)S(1)} copy-done((f32[1,5,4,128,128]{4,3,2,1,0:T(8,128)S(1)}, f32[1,5,4,128,128]{4,3,2,1,0:T(8,128)}, u32[]{:S(2)}) %copy-start) | copy-done | bytes 1310744
  2.7 0.0 copy-start.1
  2.7 1.1 %copy-done.1 = f32[1,2,5,128,128]{4,3,2,1,0:T(8,128)S(1)} copy-done((f32[1,2,5,128,128]{4,3,2,1,0:T(8,128)S(1)}, f32[1,2,5,128,128]{4,3,2,1,0:T(8,128)}, u32[]{:S(2)}) %copy-start.1) | copy-done | bytes 655384
  3.8 0.0 copy-start.2
  3.8 0.9 copy-done.2
  4.7 0.0 copy-start.3
  4.7 0.9 copy-done.3
  5.6 0.0 copy-start.4
  5.6 0.8 copy-done.4
  6.4 0.0 copy-start.5
  6.4 0.7 copy-done.5
  7.1 0.0 copy-start.6
  7.1 0.7 copy-done.6
  7.7 0.0 copy-start.7
  7.7 0.7 copy-done.7
  8.4 0.0 copy-start.8
  8.4 0.7 copy-done.8
  9.0 87.9 %shard_map.109 = f32[5,4,128,128]{3,2,1,0:T(8,128)S(1)} custom-call(f32[5,4,128,128]{3,2,1,0:T(8,128)S(1)} %bitcast.16, f32[2,128,128]{2,1,0:T(8,128)S(1)} %copy-done.3, f32[64,64]{1,0:T(8,128)S(1)} %copy-done.4, f32[2,5,128,128]{3,2,1,0:T(8,128)S(1)} %bitcast.17, f32[5,64,64]{2,1,0:T(8,128)S(1)} %bitcast.18, f32[25,1,7]{2,1,0:T(1,128)S(1)} %reshape.5.mixers, ...), custom_call_target="tpu_custom_call" | custom-call | tf_op jit(solution)/shard_map/pallas_call | solution.py:465
  96.9 1.1 %copy.21 = f32[1,5,4,128,128]{4,3,2,1,0:T(8,128)} copy(f32[1,5,4,128,128]{4,3,2,1,0:T(8,128)S(1)} %bitcast.15) | data formatting | bytes 2621440
  (1 shorter events, 0.0 us)
Async XLA Ops:
  1.4 1.3 %copy-start = (f32[1,5,4,128,128]{4,3,2,1,0:T(8,128)S(1)}, f32[1,5,4,128,128]{4,3,2,1,0:T(8,128)}, u32[]{:S(2)}) copy-start(f32[1,5,4,128,128]{4,3,2,1,0:T(8,128)} %param.11) | copy-start | bytes 3932164
  2.7 1.1 %copy-start.1 = (f32[1,2,5,128,128]{4,3,2,1,0:T(8,128)S(1)}, f32[1,2,5,128,128]{4,3,2,1,0:T(8,128)}, u32[]{:S(2)}) copy-start(f32[1,2,5,128,128]{4,3,2,1,0:T(8,128)} %param.14) | copy-start | bytes 1966084
  3.8 0.9 copy-start.2
  4.7 0.9 copy-start.3
  5.6 0.8 copy-start.4
  6.4 0.7 copy-start.5
  7.1 0.7 copy-start.6
  7.7 0.7 copy-start.7
  8.4 0.7 copy-start.8

commit v2 on v1

--- a/solution.py
+++ b/solution.py
@@ -29,10 +29,10 @@
     )
 
 
-def left_mul(w, x):
+def left_mul(rows, x):
     high, low = split(x)
-    both = dot(left_rows(w), jnp.concatenate([high, low], 0))
-    half = w.shape[0]
+    both = dot(rows, jnp.concatenate([high, low], 0))
+    half = x.shape[0]
     return both[:half] + both[half:]
 
 
@@ -69,7 +69,7 @@
     out,
     q, deriv, deriv_z, inverse, inverse_z, receivers, donors, pairs, weights,
     req_out, req_in, q_strips, q_both, q_turned, ddx, ddy, part, part_strips, is_receiver,
-    lines, ret_out, ret_in, choose, place,
+    lines, ret_out, ret_in, choose, place, rows_z, rows_y, columns_x,
     part_turned, zed, mixed, turned_back, back, step_a, step_b,
     load_sem, local_sem, req_sem, q_sem,
     ret_send, ret_recv, part_send, part_recv, back_send, back_recv,
@@ -210,13 +210,23 @@
         lines[v] = (both[:named, :LANES] + both[:named, LANES:]) + both[named:, :LANES]
         return carry
 
-    lax.fori_loop(0, VARS, interpolate, 0)
+    lax.fori_loop(0, VARS, interpolate, 0, unroll=True)
 
     def returned(g):
         return pl.ds(g * capacity, capacity)
 
     other_lines = pl.ds(0, named - capacity)
     own_lines = []
+
+    def send_lines(a):
+        def send(g):
+            pltpu.make_async_remote_copy(
+                src_ref=ret_out.at[a, g], dst_ref=ret_in.at[a, returned(zone)],
+                send_sem=ret_send.at[a], recv_sem=ret_recv.at[a], device_id={"zone": g},
+            ).start()
+
+        over_zone(send)
+
     for a in range(VARS):
         first = 3 * capacity + a * VARS
         scale = [
@@ -229,13 +239,7 @@
                 total += scale[v] * lines[v, at]
             ret_out[a, :, n] = total.reshape(groups, 1, LANES)
 
-        def send_lines(g):
-            pltpu.make_async_remote_copy(
-                src_ref=ret_out.at[a, g], dst_ref=ret_in.at[a, returned(zone)],
-                send_sem=ret_send.at[a], recv_sem=ret_recv.at[a], device_id={"zone": g},
-            ).start()
-
-        over_zone(send_lines)
+        send_lines(a)
         copy = pltpu.make_async_copy(
             ret_out.at[a, zone], ret_in.at[a, returned(zone)], local_sem.at[2 + a]
         )
@@ -320,8 +324,10 @@
             [ref[v, pl.ds(j, depth, stride=width), :] for j in range(width)], 1
         )
 
+    third_rows = left_rows(deriv_z[...])
+
     def derive_z(v, carry):
-        zed[v] = left_mul(deriv_z[...], whole_lines(q_turned, v))
+        zed[v] = left_mul(third_rows, whole_lines(q_turned, v))
         return carry
 
     lax.fori_loop(0, VARS, derive_z, 0)
@@ -340,6 +346,15 @@
 
     lax.fori_loop(0, width * (depth // levels), residual_z, 0)
     moves[7].wait()
+    moves[8].wait()
+
+    def prepare(v, carry):
+        rows_z[v] = left_rows(inverse_z[v])
+        rows_y[v] = left_rows(inverse[1, v])
+        columns_x[v] = right_columns(inverse[0, v].T)
+        return carry
+
+    lax.fori_loop(0, VARS, prepare, 0)
 
     def add_source(a):
         wait_for(ret_in.at[a, other_lines], ret_recv.at[a])
@@ -358,7 +373,7 @@
 
     def solve_z(a):
         wait_for(part_turned.at[a, others], part_recv.at[a])
-        solved = left_mul(inverse_z[a], whole_lines(part_turned, a) + mixed[a])
+        solved = left_mul(rows_z[a], whole_lines(part_turned, a) + mixed[a])
         for j in range(width):
             turned_back[a, pl.ds(j, depth, stride=width), :] = solved[:, j * LANES:(j + 1) * LANES]
 
@@ -383,7 +398,6 @@
     lax.fori_loop(1, VARS, source_and_solve, 0)
     solve_z(VARS - 1)
 
-    moves[8].wait()
     for a in range(VARS - 1):
         wait_for(turned_back.at[a, others], back_recv.at[a])
     last = VARS - 1
@@ -407,12 +421,12 @@
         x = jnp.concatenate(
             [x[:, k * width:(k + 1) * width, :].reshape(edge, LANES) for k in range(planes)], 1
         )
-        both = left_mul(inverse[1, v], x)
+        both = left_mul(rows_y[v], x)
         for k in range(planes):
             step_a[v, k * edge:(k + 1) * edge] = both[:, k * LANES:(k + 1) * LANES]
         return carry
 
-    lax.fori_loop(0, VARS, solve_y, 0)
+    lax.fori_loop(0, VARS, solve_y, 0, unroll=True)
 
     def mix_second(n, carry):
         at = pl.ds(pl.multiple_of(n * tile, tile), tile)
@@ -424,10 +438,10 @@
     lax.fori_loop(0, rows // tile, mix_second, 0)
 
     def solve_x(v, carry):
-        ddy[v] = right_mul(ddx[v], right_columns(inverse[0, v].T))
-        return carry
-
-    lax.fori_loop(0, VARS, solve_x, 0)
+        ddy[v] = right_mul(ddx[v], columns_x[v])
+        return carry
+
+    lax.fori_loop(0, VARS, solve_x, 0, unroll=True)
 
     def mix_last(n, carry):
         at = pl.ds(pl.multiple_of(n * tile, tile), tile)
@@ -492,6 +506,9 @@
             pltpu.VMEM((VARS, padded, 1, LANES), f32),
             pltpu.VMEM((2 * named, rows), bf16),
             pltpu.VMEM((rows, padded), bf16),
+            pltpu.VMEM((VARS, 2 * depth, 2 * depth), bf16),
+            pltpu.VMEM((VARS, 2 * edge, 2 * edge), bf16),
+            pltpu.VMEM((VARS, 2 * LANES, 2 * LANES), bf16),
             pltpu.VMEM((VARS, depth * width, LANES), f32),
             pltpu.VMEM((VARS, depth, width * LANES), f32),
             pltpu.VMEM((VARS, depth, width * LANES), f32),
@@ -505,7 +522,7 @@
             dma((2,)),
         ] + [dma((VARS,))] * 6,
         compiler_params=pltpu.CompilerParams(
-            collective_id=0, has_side_effects=True, vmem_limit_bytes=48 * 2**20
+            collective_id=0, has_side_effects=True, vmem_limit_bytes=56 * 2**20
         ),
     )(
         flow_state[0], derivative, derivative_z, line_inverse[0], line_inverse_z[0],

time: 98.3 us -> 90.8 us (0.924)
  local copies, waits for them, and re-layouts: 9.41 us -> 3.83 us
  Pallas kernels: 87.9 us -> 86 us
    unnamed x20 -> x2, local copies, waits for them, and re-layouts: 9.39 us -> 3.21 us
    pallas_call x1, Pallas kernels: 87.9 us -> 86 us  [local(): pl.pallas_call(functools.partial(kernel, capacity), out_shape=jax.ShapeDt...]
where the time goes in v2:
time: 90.8 us; the launch traced here: 90.5 us
  Pallas kernels  86 us (95%)
  local copies, waits for them, and re-layouts  3.83 us (4%)
    pallas_call x1, Pallas kernels, local(): pl.pallas_call(functools.partial(kernel, capacity), out_shape=jax.ShapeDt...  86 us
    unnamed x2, local copies, waits for them, and re-layouts  3.21 us

profile of v2, /device:TPU:1, one launch (start us, length us, event | category | flops | bytes accessed | tf_op | source)
XLA Modules:
  0.0 90.5 jit_solution(9373545220069240662)
XLA Ops:
  0.7 0.7 copy.18
  1.4 0.6 reshape.5.mixers
  2.0 86.0 %shard_map.109 = f32[5,4,128,128]{3,2,1,0:T(8,128)} custom-call(f32[5,4,128,128]{3,2,1,0:T(8,128)} %bitcast.16, f32[2,128,128]{2,1,0:T(8,128)} %deriv_hbm.1, f32[64,64]{1,0:T(8,128)} %deriv_z_hbm.1, f32[2,5,128,128]{3,2,1,0:T(8,128)} %bitcast.17, f32[5,64,64]{2,1,0:T(8,128)} %bitcast.18, f32[25,1,7]{2,1,0:T(1,128)} %reshape.5.mixers, s32[1]{0:T(128)S(6)} %copy.20.size, ...), custom_call_target="tpu_custom_call" | custom-call | tf_op jit(solution)/shard_map/pallas_call | solution.py:479
  88.0 2.5 %copy.21 = f32[1,5,4,128,128]{4,3,2,1,0:T(8,128)} copy(f32[1,5,4,128,128]{4,3,2,1,0:T(8,128)} %bitcast.15) | data formatting | bytes 2621440

commit v3 on v2

--- a/solution.py
+++ b/solution.py
@@ -68,7 +68,7 @@
     receivers_hbm, donors_hbm, pairs_hbm, weights_hbm,
     out,
     q, deriv, deriv_z, inverse, inverse_z, receivers, donors, pairs, weights,
-    req_out, req_in, q_strips, q_both, q_turned, ddx, ddy, part, part_strips, is_receiver,
+    req_out, req_in, told_all, q_strips, q_both, q_turned, ddx, ddy, part, part_strips, is_receiver,
     lines, ret_out, ret_in, choose, place, rows_z, rows_y, columns_x,
     part_turned, zed, mixed, turned_back, back, step_a, step_b,
     load_sem, local_sem, req_sem, q_sem,
@@ -78,7 +78,7 @@
     zone, line = lax.axis_index("zone"), lax.axis_index("line")
 
     def mix(m, a, v):
-        return mixers[a * VARS + v, 0, m]
+        return mixers[a, v, m]
 
     moves = [
         pltpu.make_async_copy(source, target, load_sem.at[n])
@@ -151,7 +151,7 @@
     own_mixer = jnp.zeros((1, LANES), f32)
     for n in range(VARS * VARS):
         at = iota((1, LANES), 1) == 3 * capacity + n
-        own_mixer = jnp.where(at, mixers[n, 0, 3], own_mixer)
+        own_mixer = jnp.where(at, mixers[n // VARS, n % VARS, 3], own_mixer)
     req_out[...] = (pick(asks, told) + own_mixer).reshape(groups, 1, LANES)
     moves[3].wait()
 
@@ -195,15 +195,24 @@
     own_request.wait()
     wait_for(req_in.at[pl.ds(0, groups - 1)], req_sem.at[1])
     asked = req_in[...].reshape(groups, LANES)
+    for n in range(3 * capacity + VARS * VARS):
+        told_all[n] = jnp.broadcast_to(asked[:, n:n + 1], (groups, LANES))
     cell_line = iota((groups, rows), 1).astype(f32)
-    for n in range(capacity):
-        share = asked[:, 2 * capacity + n:2 * capacity + n + 1]
+
+    def wide(x):
+        return jnp.concatenate([x] * (rows // LANES), 1) if rows >= LANES else x[:, :rows]
+
+    def weigh(n, carry):
+        share = wide(told_all[2 * capacity + n])
         high, low = split(
-            jnp.where(cell_line == asked[:, n:n + 1], share, 0.0)
-            + jnp.where(cell_line == asked[:, capacity + n:capacity + n + 1], 1.0 - share, 0.0)
+            jnp.where(cell_line == wide(told_all[n]), share, 0.0)
+            + jnp.where(cell_line == wide(told_all[capacity + n]), 1.0 - share, 0.0)
         )
-        choose[n * groups:(n + 1) * groups] = high
-        choose[named + n * groups:named + (n + 1) * groups] = low
+        choose[pl.ds(pl.multiple_of(n * groups, groups), groups)] = high
+        choose[pl.ds(pl.multiple_of(named + n * groups, groups), groups)] = low
+        return carry
+
+    lax.fori_loop(0, capacity, weigh, 0)
 
     def interpolate(v, carry):
         both = dot(choose[...], q_both[v])
@@ -216,22 +225,14 @@
         return pl.ds(g * capacity, capacity)
 
     other_lines = pl.ds(0, named - capacity)
-    own_lines = []
-
-    def send_lines(a):
-        def send(g):
-            pltpu.make_async_remote_copy(
-                src_ref=ret_out.at[a, g], dst_ref=ret_in.at[a, returned(zone)],
-                send_sem=ret_send.at[a], recv_sem=ret_recv.at[a], device_id={"zone": g},
-            ).start()
-
-        over_zone(send)
-
-    for a in range(VARS):
-        first = 3 * capacity + a * VARS
-        scale = [
-            jnp.broadcast_to(asked[:, first + v:first + v + 1], (groups, LANES)) for v in range(VARS)
-        ]
+
+    def own_lines(a):
+        return pltpu.make_async_copy(
+            ret_out.at[a, zone], ret_in.at[a, returned(zone)], local_sem.at[2 + a]
+        )
+
+    def send_lines(a, carry):
+        scale = [told_all[3 * capacity + a * VARS + v] for v in range(VARS)]
         for n in range(capacity):
             at = slice(n * groups, (n + 1) * groups)
             total = scale[0] * lines[0, at]
@@ -239,12 +240,17 @@
                 total += scale[v] * lines[v, at]
             ret_out[a, :, n] = total.reshape(groups, 1, LANES)
 
-        send_lines(a)
-        copy = pltpu.make_async_copy(
-            ret_out.at[a, zone], ret_in.at[a, returned(zone)], local_sem.at[2 + a]
-        )
-        copy.start()
-        own_lines.append(copy)
+        def send(g):
+            pltpu.make_async_remote_copy(
+                src_ref=ret_out.at[a, g], dst_ref=ret_in.at[a, returned(zone)],
+                send_sem=ret_send.at[a], recv_sem=ret_recv.at[a], device_id={"zone": g},
+            ).start()
+
+        over_zone(send)
+        own_lines(a).start()
+        return carry
+
+    lax.fori_loop(0, VARS, send_lines, 0)
 
     moves[4].wait()
     slot_of = donor * capacity + position
@@ -357,6 +363,7 @@
     lax.fori_loop(0, VARS, prepare, 0)
 
     def add_source(a):
+        own_lines(a).wait()
         wait_for(ret_in.at[a, other_lines], ret_recv.at[a])
         high, low = split(ret_in[a].reshape(padded, LANES))
         both = dot(place[...], jnp.concatenate([high, low], 1))
@@ -386,17 +393,18 @@
         over_line(send_back)
         back[a, line] = turned_back[a, level(line)]
 
-    for copy in own_lines:
-        copy.wait()
-    add_source(0)
-
     def source_and_solve(a, carry):
-        add_source(a)
-        solve_z(a - 1)
-        return carry
-
-    lax.fori_loop(1, VARS, source_and_solve, 0)
-    solve_z(VARS - 1)
+        @pl.when(a < VARS)
+        def _():
+            add_source(a)
+
+        @pl.when(a > 0)
+        def _():
+            solve_z(a - 1)
+
+        return carry
+
+    lax.fori_loop(0, VARS + 1, source_and_solve, 0)
 
     for a in range(VARS - 1):
         wait_for(turned_back.at[a, others], back_recv.at[a])
@@ -417,7 +425,7 @@
     wait_for(turned_back.at[last, others], back_recv.at[last])
 
     def solve_y(v, carry):
-        x = step_b[v] + mixers[v * VARS + last, 0, 4] * back[last]
+        x = step_b[v] + mixers[v, last, 4] * back[last]
         x = jnp.concatenate(
             [x[:, k * width:(k + 1) * width, :].reshape(edge, LANES) for k in range(planes)], 1
         )
@@ -493,6 +501,7 @@
             pltpu.VMEM((1, slots), f32),
             pltpu.VMEM((groups, 1, LANES), f32),
             pltpu.VMEM((groups, 1, LANES), f32),
+            pltpu.VMEM((3 * capacity + VARS * VARS, groups, LANES), f32),
             pltpu.VMEM((VARS, blocks, planes * width, LANES), f32),
             pltpu.VMEM((VARS, rows, 2 * LANES), bf16),
             pltpu.VMEM((VARS, depth * width, LANES), f32),
@@ -522,13 +531,12 @@
             dma((2,)),
         ] + [dma((VARS,))] * 6,
         compiler_params=pltpu.CompilerParams(
-            collective_id=0, has_side_effects=True, vmem_limit_bytes=56 * 2**20
+            collective_id=0, has_side_effects=True, vmem_limit_bytes=48 * 2**20
         ),
     )(
-        flow_state[0], derivative, derivative_z, line_inverse[0], line_inverse_z[0],
-        jnp.transpose(mixers[0], (1, 2, 0)).reshape(VARS * VARS, 1, mixers.shape[1]),
-        zone_size, receiver_line[0], donor_group[0, :, :, 0], donor_line[0, 0].T,
-        stencil_weight[0],
+        *(pltpu.with_memory_space_constraint(x, pltpu.HBM) for x in (flow_state[0], derivative, derivative_z, line_inverse[0], line_inverse_z[0])),
+        jnp.transpose(mixers[0], (1, 2, 0)), zone_size,
+        *(pltpu.with_memory_space_constraint(x, pltpu.HBM) for x in (receiver_line[0], donor_group[0, :, :, 0], donor_line[0, 0].T, stencil_weight[0])),
     )
     return result[None]
 

time: 90.8 us -> 87.6 us (0.965)
  local copies, waits for them, and re-layouts: 3.83 us -> 1.77 us
  Pallas kernels: 86 us -> 84.9 us
    unnamed x2, local copies, waits for them, and re-layouts: 3.21 us -> 1.77 us
    pallas_call x1, Pallas kernels: 86 us -> 84.9 us  [local(): pl.pallas_call(functools.partial(kernel, capacity), out_shape=jax.ShapeDt...]
where the time goes in v3:
time: 87.6 us; the launch traced here: 87.4 us
  Pallas kernels  84.9 us (97%)
  local copies, waits for them, and re-layouts  1.77 us (2%)
    pallas_call x1, Pallas kernels, local(): pl.pallas_call(functools.partial(kernel, capacity), out_shape=jax.ShapeDt...  84.9 us
    unnamed x2, local copies, waits for them, and re-layouts  1.77 us

profile of v3, /device:TPU:1, one launch (start us, length us, event | category | flops | bytes accessed | tf_op | source)
XLA Modules:
  0.0 87.4 jit_solution(17685244653507191413)
XLA Ops:
  0.7 0.7 copy.14
  1.4 84.9 %shard_map.109 = f32[5,4,128,128]{3,2,1,0:T(8,128)S(1)} custom-call(f32[5,4,128,128]{3,2,1,0:T(8,128)} %bitcast.17, f32[2,128,128]{2,1,0:T(8,128)} %deriv_hbm.1, f32[64,64]{1,0:T(8,128)} %deriv_z_hbm.1, f32[2,5,128,128]{3,2,1,0:T(8,128)} %bitcast.18, f32[5,64,64]{2,1,0:T(8,128)} %bitcast.19, f32[5,5,7]{2,1,0:T(8,128)S(1)} %bitcast.16, s32[1]{0:T(128)S(6)} %copy.16.size, ...), custom_call_target="tpu_custom_call" | custom-call | tf_op jit(solution)/shard_map/pallas_call | solution.py:487
  86.3 1.1 %copy.17 = f32[1,5,4,128,128]{4,3,2,1,0:T(8,128)} copy(f32[1,5,4,128,128]{4,3,2,1,0:T(8,128)S(1)} %bitcast.15) | data formatting | bytes 2621440

commit v4 on v3

--- a/solution.py
+++ b/solution.py
@@ -88,7 +88,7 @@
             (inverse_z_hbm, inverse_z), (inverse_hbm, inverse),
         ))
     ]
-    for move in moves:
+    for move in moves[:3]:
         move.start()
     planes, edge = q.shape[1], q.shape[2]
     rows = planes * edge
@@ -100,18 +100,28 @@
     padded = ret_in.shape[1]
 
     def over_zone(body):
-        def step(s, carry):
-            body(lax.rem(zone + s, groups))
+        def step(n, carry):
+            turn = lax.rem(n, 2)
+            offset = groups // 2 + (n + turn) // 2 * (2 * turn - 1)
+            body(lax.rem(zone + (offset if groups % 2 == 0 else n + 1), groups))
             return carry
 
-        lax.fori_loop(1, groups, step, 0)
+        lax.fori_loop(0, groups - 1, step, 0)
+
+    side = next((n for n in (2, 3, 4, 8) if n * n == blocks), 1)
+    tall = blocks // side
+
+    def hops(step):
+        return min(step[0], tall - step[0]) + min(step[1], side - step[1])
+
+    steps = sorted(
+        ((y, x) for y in range(tall) for x in range(side) if (y, x) != (0, 0)),
+        key=lambda step: (-hops(step), sorted((min(step[0], tall - step[0]), min(step[1], side - step[1])))),
+    )
 
     def over_line(body):
-        def step(s, carry):
-            body(lax.rem(line + s, blocks))
-            return carry
-
-        lax.fori_loop(1, blocks, step, 0)
+        for y, x in steps:
+            body(lax.rem(line // side + y, tall) * side + lax.rem(line + x, side))
 
     def strips(x):
         x = x.reshape(planes, blocks, width, LANES)
@@ -128,6 +138,8 @@
     barrier = pltpu.get_barrier_semaphore()
     over_zone(lambda g: pl.semaphore_signal(barrier, inc=1, device_id={"zone": g}))
     over_line(lambda t: pl.semaphore_signal(barrier, inc=1, device_id={"line": t}))
+    for move in moves[3:]:
+        move.start()
 
     diagonal = iota((slots, slots), 0) == iota((slots, slots), 1)
 
@@ -153,13 +165,6 @@
         at = iota((1, LANES), 1) == 3 * capacity + n
         own_mixer = jnp.where(at, mixers[n // VARS, n % VARS, 3], own_mixer)
     req_out[...] = (pick(asks, told) + own_mixer).reshape(groups, 1, LANES)
-    moves[3].wait()
-
-    def cut_state(v, carry):
-        q_strips[v] = strips(q[v])
-        return carry
-
-    lax.fori_loop(0, VARS, cut_state, 0)
 
     pl.semaphore_wait(barrier, groups + blocks - 2)
 
@@ -172,6 +177,13 @@
     over_zone(send_request)
     own_request = pltpu.make_async_copy(req_out.at[zone], req_in.at[zone], local_sem.at[0])
     own_request.start()
+    moves[3].wait()
+
+    def cut_state(v, carry):
+        q_strips[v] = strips(q[v])
+        return carry
+
+    lax.fori_loop(0, VARS, cut_state, 0)
 
     def send_state(t):
         pltpu.make_async_remote_copy(

time: 87.6 us -> 83.8 us (0.957)
  Pallas kernels: 84.9 us -> 81 us
    pallas_call x1, Pallas kernels: 84.9 us -> 81 us  [local(): pl.pallas_call(functools.partial(kernel, capacity), out_shape=jax.ShapeDt...]
where the time goes in v4:
time: 83.8 us; the launch traced here: 83.4 us
  Pallas kernels  81 us (97%)
  local copies, waits for them, and re-layouts  1.77 us (2%)
    pallas_call x1, Pallas kernels, local(): pl.pallas_call(functools.partial(kernel, capacity), out_shape=jax.ShapeDt...  81 us
    unnamed x2, local copies, waits for them, and re-layouts  1.77 us

profile of v4, /device:TPU:1, one launch (start us, length us, event | category | flops | bytes accessed | tf_op | source)
XLA Modules:
  0.0 83.4 jit_solution(9986646542800231617)
XLA Ops:
  0.7 0.7 copy.14
  1.4 81.0 %shard_map.109 = f32[5,4,128,128]{3,2,1,0:T(8,128)S(1)} custom-call(f32[5,4,128,128]{3,2,1,0:T(8,128)} %bitcast.17, f32[2,128,128]{2,1,0:T(8,128)} %deriv_hbm.1, f32[64,64]{1,0:T(8,128)} %deriv_z_hbm.1, f32[2,5,128,128]{3,2,1,0:T(8,128)} %bitcast.18, f32[5,64,64]{2,1,0:T(8,128)} %bitcast.19, f32[5,5,7]{2,1,0:T(8,128)S(1)} %bitcast.16, s32[1]{0:T(128)S(6)} %copy.16.size, ...), custom_call_target="tpu_custom_call" | custom-call | tf_op jit(solution)/shard_map/pallas_call | solution.py:499
  82.3 1.1 %copy.17 = f32[1,5,4,128,128]{4,3,2,1,0:T(8,128)} copy(f32[1,5,4,128,128]{4,3,2,1,0:T(8,128)S(1)} %bitcast.15) | data formatting | bytes 2621440
